TPU v7x, 32 devices: a whole 2x2x4 slice. The times are simulated.
32 devices in a mesh: space: 4 (over z), agg: 8 (over y, x, core).
Axes of the slice: x: 2, y: 2, z: 4, core: 2. Of those that a mesh axis runs over, the one named last changes fastest.
Arguments:
- h_blocks: bfloat16 [4096, 7, 64, 64], P(('space', 'agg')), may hold values from -2.5 to 2.5
- h_cols: int32 [4096, 7], P(('space', 'agg')), may hold values from 0 to 4095, as said below
- p_blocks: bfloat16 [4096, 64, 64], P(('space', 'agg')), may hold values from -0.75 to 0.75
- agg_map: int32 [4096], P(('space', 'agg')), may hold values from 0 to 15, as said below
- term_slot: int32 [4096, 7], P(('space', 'agg')), may hold values from 0 to 6
- owner_pos: int32 [512], P(('space', 'agg')), may hold values from 0 to 511, as said below
Outputs:
- coarse: bfloat16 [512, 7, 64, 64], P(('space', 'agg'))
Inputs may be any that keep to these rules, and one draw needn't show every extreme that they name: h_cols[e, 0] = e. Every other entry names an element of the same device, except that for an element among the first 32 of its device (not in the lowest slab) entry 1 names one of the last 32 elements of the device one step lower along space with the same agg index, and for one among the last 32 (not in the highest slab) entry 2 names one of the first 32 elements of the device one step higher along space with the same agg index. `agg_map`: each device's elements form 16 aggregates of exactly 8 elements. `owner_pos`: A permutation of the coarse rows that keeps each space slab: the rows of slab s go to rows s * 128 to (s + 1) * 128 - 1. The owner of output row q is agg index (q % 128) // 16. The 16 rows of one device go to every owner of its slab, exactly 2 to each.
All inputs are finite; a program needn't handle non-finite values.
Results may differ from a plain program's by a relative error of at most 0.0049.
Values may be sent and summed in bfloat16 or wider, within the bound.
A program may use at most 256 MiB of HBM per device.

v0:
```python
import jax
import jax.numpy as jnp
from jax import lax
from jax.sharding import PartitionSpec as P

KC = 7


def extended(array, sides, width):
    for axis, dim in sides:
        peers, length = (lax.axis_size(axis), array.shape[dim])
        up = [(i, (i + 1) % peers) for i in range(peers - 1)]
        down = [(j, i) for i, j in up]
        last = lax.slice_in_dim(array, length - width, length, axis=dim)
        initial = lax.slice_in_dim(array, 0, width, axis=dim)
        before = lax.ppermute(last, axis, up)
        after = lax.ppermute(initial, axis, down)
        array = jnp.concatenate([before, array, after], axis=dim)
    return array


def body(h_blocks, h_cols, p_blocks, agg_map, term_slot, owner_pos):
    rows_dev = p_blocks.shape[0]
    face = rows_dev // 4
    block_size = p_blocks.shape[1]
    coarse_width = KC
    aggs_dev = owner_pos.shape[0]
    n_agg = lax.axis_size("agg")
    device = lax.axis_index("space") * n_agg + lax.axis_index("agg")
    padded = extended(p_blocks, (("space", 0),), face)
    source_dev = h_cols // rows_dev
    source_row = h_cols % rows_dev
    lookup = jnp.where(
        source_dev == device,
        face + source_row,
        jnp.where(
            source_dev < device, source_row - (rows_dev - face), face + rows_dev + source_row
        ),
    )
    gathered = jnp.take(padded, lookup, axis=0)
    hp_part = jnp.einsum(
        "ekij,ekjl->ekil", h_blocks, gathered, preferred_element_type=jnp.float32
    ).astype(jnp.bfloat16)
    terms = jnp.einsum("eji,ekjl->ekil", p_blocks, hp_part, preferred_element_type=jnp.float32)
    target = (agg_map[:, None] * coarse_width + term_slot).reshape(-1)
    summed = jax.ops.segment_sum(
        terms.reshape(-1, block_size, block_size), target, num_segments=aggs_dev * coarse_width
    )
    local_rows = summed.reshape(aggs_dev, coarse_width, block_size, block_size).astype(jnp.bfloat16)
    slab_rows = aggs_dev * n_agg
    in_slab = owner_pos % slab_rows
    slab_part = jnp.zeros((slab_rows, coarse_width, block_size, block_size), jnp.float32)
    slab_part = slab_part.at[in_slab].set(local_rows.astype(jnp.float32))
    owned = lax.psum_scatter(slab_part.astype(jnp.bfloat16), "agg", scatter_dimension=0, tiled=True)
    return owned


def solution(mesh):
    placed = (
        P(("space", "agg"), None, None, None),
        P(("space", "agg"), None),
        P(("space", "agg"), None, None),
        P(("space", "agg")),
        P(("space", "agg"), None),
        P(("space", "agg")),
    )
    return jax.shard_map(
        body,
        mesh=mesh,
        in_specs=placed,
        out_specs=P(("space", "agg"), None, None, None),
        check_vma=False,
    )
```

profile of v0, /device:TPU:0, one launch (start us, length us, event | category | flops | bytes accessed | tf_op | source)
XLA Modules:
  0.0 426.1 jit_solution(15723553120672045572)
XLA Ops:
  6.5 4.0 copy.11
  10.6 1.1 fusion.16
  11.7 5.7 %collective-permute-start = (bf16[32,64,64]{2,1,0:T(8,128)(2,1)}, bf16[32,64,64]{2,1,0:T(8,128)(2,1)}, u32[]{:S(2)}, u32[]{:S(2)}) collective-permute-start(bf16[32,64,64]{2,1,0:T(8,128)(2,1)} %get-tuple-element.7), channel_id=1, source_target_pairs={{0,8},{8,16},{16,24},{1,9},{9,17},{17,25},{2,10},{10,18},{18,26},{... | collective-permute-start | bytes 786440 | tf_op jit(solution)/shard_map/ppermute | solution.py:16
  17.4 1.3 collective-permute-start.1
  18.7 0.7 compare_and_fusion
  19.5 0.2 reshape.18
  19.7 0.7 broadcast_multiply_fusion
  20.4 0.7 broadcast_add_fusion
  21.1 0.1 copy.10
  21.2 25.8 %copy.17 = bf16[128,7,64,64]{2,3,1,0:T(8,128)(2,1)} copy(bf16[128,7,64,64]{0,3,2,1:T(8,128)(2,1)} %param.6) | data formatting | bytes 14680064 | tf_op args[0]
  47.1 3.7 copy.18
  50.9 0.2 reshape.26
  51.2 2.2 pad_maximum_fusion
  53.4 22.8 %gather_fusion = bf16[896,64,64]{2,1,0:T(8,128)(2,1)} fusion(bf16[192,64,64]{2,1,0:T(8,128)(2,1)S(1)} %pad_maximum_fusion, s32[1024]{0:T(1024)S(1)} %pad_clamp_fusion), kind=kCustom, calls=%fused_computation | custom fusion | bytes 14683648 | tf_op jit(solution)/shard_map/jit(_take)/gather | solution.py:40
  76.2 24.8 %fusion = f32[128,7,64,64]{3,2,1,0:T(8,128)} fusion(bf16[128,64,64,1]{2,1,3,0:T(8,128)(2,1)} %copy.18, bf16[128,7,64,64]{2,3,1,0:T(8,128)(2,1)} %copy.17, bf16[128,7,64,64]{3,2,1,0:T(8,128)(2,1)} %bitcast.13, pred[128,7]{1,0:T(8,128)(4,1)S(1)} %copy.10), kind=kOutput, calls=%fused_computation.3 | convolution fusion | flops 946864128 | bytes 30409600 | tf_op jit(solution)/shard_map/eji,ekjl->ekil/dot_general | solution.py:44
  101.0 29.6 %copy.16 = f32[896,64,64]{2,1,0:T(8,128)} copy(f32[896,64,64]{1,2,0:T(8,128)} %bitcast.12) | data formatting | bytes 29360128 | tf_op jit(solution)/shard_map/reshape | solution.py:47
  130.6 2.2 broadcast_in_dim.24
  132.8 137.5 %scatter_fusion = f32[112,64,64]{2,1,0:T(8,128)} fusion(f32[112,64,64]{2,1,0:T(8,128)} %broadcast_in_dim.24, s32[896]{0:T(1024)S(1)} %reshape.26, f32[896,64,64]{2,1,0:T(8,128)} %copy.16), kind=kCustom, calls=%fused_computation.1 | custom fusion | flops 3670016 | bytes 44043776 | tf_op jit(solution)/shard_map/scatter-add | solution.py:46
  270.3 2.4 convert_element_type.21
  272.7 2.2 convert.1
  274.9 13.4 %broadcast_in_dim.22 = f32[128,7,64,64]{3,2,1,0:T(8,128)} broadcast(f32[]{:T(128)} %constant.58.clone.1), dimensions={} | broadcast | bytes 14680068 | tf_op jit(solution)/shard_map/broadcast_in_dim | solution.py:52
  288.4 7.7 %scatter_fusion.1 = f32[128,7,64,64]{3,2,1,0:T(8,128)} fusion(f32[128,7,64,64]{3,2,1,0:T(8,128)} %broadcast_in_dim.22, s32[16]{0:T(128)S(1)} %compare_select_fusion.1, f32[16,7,64,64]{3,2,1,0:T(8,128)} %convert.1), kind=kCustom, calls=%fused_computation.2 | custom fusion | bytes 5505088 | tf_op jit(solution)/shard_map/scatter | solution.py:53
  296.1 17.3 %convert_element_type.24 = bf16[128,7,64,64]{3,2,1,0:T(8,128)(2,1)} convert(f32[128,7,64,64]{3,2,1,0:T(8,128)} %scatter_fusion.1) | non-fusion elementwise | flops 3670016 | bytes 22020096 | tf_op jit(solution)/shard_map/convert_element_type | solution.py:54
  313.5 105.8 %reduce-scatter.2.cloned.1.call-done = bf16[16,7,64,64]{3,2,1,0:T(8,128)(2,1)} async-done(((bf16[128,7,64,64]{3,2,1,0:T(8,128)(2,1)}), bf16[16,7,64,64]{3,2,1,0:T(8,128)(2,1)}) %reduce-scatter.2.cloned.1.call-update) | async-done | bytes 917520 | tf_op jit(solution)/shard_map/reduce_scatter | solution.py:54
  (14 shorter events, 0.3 us)
Async XLA Ops:
  6.5 40.5 %copy-start.1 = (bf16[128,64,64]{0,2,1:T(8,128)(2,1)S(1)}, bf16[128,64,64]{0,2,1:T(8,128)(2,1)}, u32[]{:S(2)}) copy-start(bf16[128,64,64]{0,2,1:T(8,128)(2,1)} %param.8) | copy-start | bytes 3145732
  6.5 44.6 %copy-start.2 = (s32[16]{0:T(128)S(1)}, s32[16]{0:T(128)}, u32[]{:S(2)}) copy-start(s32[16]{0:T(128)} %param.11) | copy-start | bytes 196
  6.5 412.7 %reduce-scatter.2.cloned.1.call-start = ((), (), s32[]{:S(2)}) async-start(), calls=%async_computation.1 | async-start | bytes 16515072 | tf_op jit(solution)/shard_map/reduce_scatter | solution.py:54
  10.6 40.6 %copy-start = (bf16[128,64,64]{2,1,0:T(8,128)(2,1)}, bf16[128,64,64]{2,1,0:T(8,128)(2,1)S(1)}, u32[]{:S(2)}) copy-start(bf16[128,64,64]{2,1,0:T(8,128)(2,1)S(1)} %copy.11) | copy-start | bytes 3145732
  11.7 39.5 %collective-permute-start = (bf16[32,64,64]{2,1,0:T(8,128)(2,1)}, bf16[32,64,64]{2,1,0:T(8,128)(2,1)}, u32[]{:S(2)}, u32[]{:S(2)}) collective-permute-start(bf16[32,64,64]{2,1,0:T(8,128)(2,1)} %get-tuple-element.7), channel_id=1, source_target_pairs={{0,8},{8,16},{16,24},{1,9},{9,17},{17,25},{2,10},{10,18},{18,26},{... | collective-permute-start | bytes 786440 | tf_op jit(solution)/shard_map/ppermute | solution.py:16
  17.4 33.8 %collective-permute-start.1 = (bf16[32,64,64]{2,1,0:T(8,128)(2,1)}, bf16[32,64,64]{2,1,0:T(8,128)(2,1)}, u32[]{:S(2)}, u32[]{:S(2)}) collective-permute-start(bf16[32,64,64]{2,1,0:T(8,128)(2,1)} %get-tuple-element.8), channel_id=1, source_target_pairs={{8,0},{16,8},{24,16},{9,1},{17,9},{25,17},{10,2},{18,10},{26,18},{... | collective-permute-start | bytes 786440 | tf_op jit(solution)/shard_map/ppermute | solution.py:17
Sparse Core Ops, SparseCore 0:
  313.6 105.6 reduce-scatter.1
where the time goes:
time: 429 us; the launch traced here: 426 us
  other arithmetic  164 us (38%)
  local copies, waits for them, and re-layouts  111 us (26%)
  waiting for transfers between devices  106 us (25%)
  matrix products  24.8 us (6%)
  between operations  13.5 us (3%)
  starting transfers between devices  6.99 us (2%)
    scatter-add x1, other arithmetic, body(): jax.ops.segment_sum(terms.reshape(-1, block_size, block_size), target, nu...  137 us
    reduce_scatter x1, waiting for transfers between devices, body(): lax.psum_scatter(slab_part.astype(jnp.bfloat16), 'agg', scatter_dimension...  106 us
    unnamed x9, local copies, waits for them, and re-layouts  33.6 us
    reshape x1, local copies, waits for them, and re-layouts, body(): terms.reshape(-1, block_size, block_size)  29.6 us
    dot_general x1, matrix products, body(): jnp.einsum('eji,ekjl->ekil', p_blocks, hp_part, preferred_element_type=jn...  24.8 us
    gather x1, local copies, waits for them, and re-layouts, body(): gathered = jnp.take(padded, lookup, axis=0)  22.8 us
    convert_element_type x1, other arithmetic, body(): slab_part.astype(jnp.bfloat16)  17.3 us
    broadcast_in_dim x1, local copies, waits for them, and re-layouts, body(): jnp.zeros((slab_rows, coarse_width, block_size, block_size), jnp.float32)  13.4 us
  transfers between devices with their start and end apart: 3, of which 1 were waited for; matrix products, arithmetic and copies ran while one was open for 8% of the time, Pallas kernels for 0%

commit v1 on v0

v1 whole, which is shorter than its diff:
```python
import functools

import jax
import jax.numpy as jnp
from jax import lax
from jax.experimental import pallas as pl
from jax.experimental.pallas import tpu as pltpu
from jax.sharding import PartitionSpec as P

KC = 7
VMEM_LIMIT = 48 * 1024 * 1024


def pair_kernel(x_ref, o_ref, turned):
    _, rows, cols, elems = x_ref.shape
    half = rows // 2
    for q in range(half):
        both = jnp.concatenate([x_ref[0, q], x_ref[0, half + q]], axis=0)
        turned[pl.ds(q * elems, elems), :] = both.T.astype(jnp.float32)
    for e in range(elems):
        o_ref[e, 0] = turned[pl.ds(e, half, stride=elems), :].astype(o_ref.dtype)


def paired(x):
    count, rows, cols, elems = x.shape
    half = rows // 2
    return pl.pallas_call(
        pair_kernel,
        grid=(count,),
        in_specs=[pl.BlockSpec((1, rows, cols, elems), lambda k: (k, 0, 0, 0))],
        out_specs=pl.BlockSpec((elems, 1, half, 2 * cols), lambda k: (0, k, 0, 0)),
        out_shape=jax.ShapeDtypeStruct((elems, count, half, 2 * cols), x.dtype),
        scratch_shapes=[pltpu.VMEM((half * elems, 2 * cols), jnp.float32)],
        compiler_params=pltpu.CompilerParams(vmem_limit_bytes=VMEM_LIMIT),
        cost_estimate=pl.CostEstimate(flops=0, bytes_accessed=4 * x.size, transcendentals=0),
    )(x)


def swap_halves(x):
    half = x.shape[-1] // 2
    return jnp.concatenate([x[:, half:], x[:, :half]], axis=1)


def galerkin_kernel(n_agg, dev_ref, cols_ref, slot_ref, agg_ref, owner_ref,
                    h_ref, before_ref, own_ref, after_ref, o_ref,
                    dense, stack, total, order, place, count):
    step = pl.program_id(0)
    elems = own_ref.shape[0]
    face = before_ref.shape[0]
    half, lanes = own_ref.shape[1:]
    size = lanes // 2
    aggs = owner_ref.shape[0]
    per_agg = elems // aggs
    cap = aggs // n_agg
    low = lax.broadcasted_iota(jnp.int32, (half, lanes), 1) < size
    low2 = lax.broadcasted_iota(jnp.int32, (size, lanes), 1) < size

    @pl.when(step == 0)
    def _():
        def clear(i, c):
            count[i] = 0
            return c
        lax.fori_loop(0, aggs + n_agg, clear, 0)

        def rank_row(r, c):
            owner = lax.rem(owner_ref[r], aggs * n_agg) // aggs
            seen = count[aggs + owner]
            count[aggs + owner] = seen + 1
            place[r] = owner * cap + seen
            return c
        lax.fori_loop(0, aggs, rank_row, 0)

        def rank_elem(e, c):
            a = agg_ref[e]
            seen = count[a]
            count[a] = seen + 1
            order[place[a] * per_agg + seen] = e
            return c
        lax.fori_loop(0, elems, rank_elem, 0)

        def spread(src, first):
            def one(c, carry):
                x = src[c].astype(jnp.float32)
                y = swap_halves(x)
                dense[first + c, 0:half] = jnp.where(low, x, 0.0).astype(jnp.bfloat16)
                dense[first + c, half:2 * half] = jnp.where(low, y, 0.0).astype(jnp.bfloat16)
                dense[first + c, 2 * half:3 * half] = jnp.where(low, 0.0, y).astype(jnp.bfloat16)
                dense[first + c, 3 * half:4 * half] = jnp.where(low, 0.0, x).astype(jnp.bfloat16)
                return carry
            lax.fori_loop(0, src.shape[0], one, 0, unroll=4)
        spread(before_ref, 0)
        spread(own_ref, face)
        spread(after_ref, face + elems)

    dev = dev_ref[0]
    base = dev * elems
    hop = n_agg * elems
    total[...] = jnp.zeros_like(total)
    for t in range(per_agg):
        e = order[step * per_agg + t]
        stack[pl.ds(t * half, half), :] = own_ref[e]
        for k in range(KC):
            x = cols_ref[k, e] - base
            c = jnp.where(x < 0, x + hop - (elems - face),
                          jnp.where(x >= elems, x - hop + face + elems, x + face))
            hp = jnp.dot(h_ref[e, k], dense[c], preferred_element_type=jnp.float32)
            total[slot_ref[k, e], pl.ds(t * half, half), :] += hp
    left = stack[...].T
    for j in range(0, KC, 2):
        if j + 1 < KC:
            right = jnp.concatenate([total[j], total[j + 1]], axis=1).astype(jnp.bfloat16)
        else:
            right = total[j].astype(jnp.bfloat16)
        r = jnp.dot(left, right, preferred_element_type=jnp.float32)
        a_top, a_bot = r[:size, :lanes], r[size:, :lanes]
        if j + 1 < KC:
            b_top, b_bot = r[:size, lanes:], r[size:, lanes:]
        else:
            b_top = b_bot = jnp.zeros_like(a_top)
        out = jnp.where(low2, a_top, b_bot) + swap_halves(jnp.where(low2, b_top, a_bot))
        o_ref[0, j // 2] = out.astype(o_ref.dtype)


def galerkin(n_agg, dev, cols, slots, agg_map, owner_pos, h, before, own, after):
    elems, _, half, lanes = h.shape
    face = before.shape[0]
    aggs = owner_pos.shape[0]
    smem = pl.BlockSpec(memory_space=pltpu.SMEM)
    vmem = pl.BlockSpec(memory_space=pltpu.VMEM)
    tiles = (KC + 1) // 2
    return pl.pallas_call(
        functools.partial(galerkin_kernel, n_agg),
        grid=(aggs,),
        in_specs=[smem] * 5 + [vmem] * 4,
        out_specs=pl.BlockSpec((1, tiles, lanes // 2, lanes), lambda g: (g, 0, 0, 0)),
        out_shape=jax.ShapeDtypeStruct((aggs, tiles, lanes // 2, lanes), jnp.bfloat16),
        scratch_shapes=[
            pltpu.VMEM((elems + 2 * face, lanes, lanes), jnp.bfloat16),
            pltpu.VMEM((elems // aggs * half, lanes), jnp.bfloat16),
            pltpu.VMEM((KC, elems // aggs * half, lanes), jnp.float32),
            pltpu.SMEM((elems,), jnp.int32),
            pltpu.SMEM((aggs,), jnp.int32),
            pltpu.SMEM((aggs + n_agg,), jnp.int32),
        ],
        compiler_params=pltpu.CompilerParams(vmem_limit_bytes=VMEM_LIMIT),
    )(dev, cols, slots, agg_map, owner_pos, h, before, own, after)


def place_kernel(n_agg, me_ref, owner_ref, x_ref, o_ref, source, count):
    rows, tiles, size, lanes = x_ref.shape
    cap = rows // n_agg
    me = me_ref[0]

    def one(i, seen):
        spot = lax.rem(owner_ref[i], rows * n_agg)
        mine = spot // rows == me

        @pl.when(mine)
        def _():
            source[lax.rem(spot, rows)] = seen
        return seen + mine.astype(jnp.int32)
    lax.fori_loop(0, rows * n_agg, one, 0)

    def row(q, carry):
        s = source[q]
        for t in range(tiles):
            x = x_ref[s, t]
            o_ref[q, 2 * t] = x[:, :size]
            if 2 * t + 1 < KC:
                o_ref[q, 2 * t + 1] = x[:, size:]
        return carry
    lax.fori_loop(0, rows, row, 0)


def placed_rows(n_agg, me, owners, x):
    rows, tiles, size, lanes = x.shape
    return pl.pallas_call(
        functools.partial(place_kernel, n_agg),
        in_specs=[pl.BlockSpec(memory_space=pltpu.SMEM)] * 2 + [pl.BlockSpec(memory_space=pltpu.VMEM)],
        out_specs=pl.BlockSpec(memory_space=pltpu.VMEM),
        out_shape=jax.ShapeDtypeStruct((rows, KC, size, size), x.dtype),
        scratch_shapes=[pltpu.SMEM((rows,), jnp.int32), pltpu.SMEM((1,), jnp.int32)],
        compiler_params=pltpu.CompilerParams(vmem_limit_bytes=VMEM_LIMIT),
    )(me, owners, x)


def body(h_blocks, h_cols, p_blocks, agg_map, term_slot, owner_pos):
    elems = p_blocks.shape[0]
    face = elems // 4
    aggs = owner_pos.shape[0]
    n_agg = lax.axis_size("agg")
    n_space = lax.axis_size("space")
    me = lax.axis_index("agg")
    device = lax.axis_index("space") * n_agg + me
    owners = lax.all_gather(owner_pos, "agg", tiled=True)

    own = paired(p_blocks.transpose(1, 2, 0)[None])[:, 0]
    up = [(i, i + 1) for i in range(n_space - 1)]
    down = [(j, i) for i, j in up]
    before = lax.ppermute(own[elems - face:], "space", up)
    after = lax.ppermute(own[:face], "space", down)
    h = paired(h_blocks.transpose(1, 2, 3, 0))
    rows = galerkin(n_agg, device.reshape(1).astype(jnp.int32), h_cols.T, term_slot.T,
                    agg_map, owner_pos, h, before, own, after)
    tail = rows.shape[1:]
    got = lax.all_to_all(rows.reshape((n_agg, aggs // n_agg) + tail), "agg", 0, 0)
    return placed_rows(n_agg, me.reshape(1).astype(jnp.int32), owners, got.reshape((aggs,) + tail))


def solution(mesh):
    placed = (
        P(("space", "agg"), None, None, None),
        P(("space", "agg"), None),
        P(("space", "agg"), None, None),
        P(("space", "agg")),
        P(("space", "agg"), None),
        P(("space", "agg")),
    )
    return jax.shard_map(
        body,
        mesh=mesh,
        in_specs=placed,
        out_specs=P(("space", "agg"), None, None, None),
        check_vma=False,
    )
```

time: 429 us -> 78.3 us (0.18)
  other arithmetic: 164 us -> 0 us
  local copies, waits for them, and re-layouts: 111 us -> 2.19 us
  waiting for transfers between devices: 106 us -> 0.01 us
  Pallas kernels: 0 us -> 47.9 us
  matrix products: 24.8 us -> 0 us
  blocking collectives: 0 us -> 16.1 us
  between operations: 13.5 us -> 0.81 us
    scatter-add x1 -> x0, other arithmetic: 137 us -> none  [body(): jax.ops.segment_sum(terms.reshape(-1, block_size, block_size), target, nu...]
    reduce_scatter x1 -> x0, waiting for transfers between devices: 106 us -> none  [body(): lax.psum_scatter(slab_part.astype(jnp.bfloat16), 'agg', scatter_dimension...]
    pallas_call x0 -> x4, Pallas kernels: none -> 47.9 us  [the longest x1 25.4 us: galerkin(): pl.pallas_call(functools.partial(galerkin_kernel, n_agg), grid=(aggs,), i...]
    unnamed x9 -> x15, local copies, waits for them, and re-layouts: 33.6 us -> 2.15 us
    reshape x1 -> x0, local copies, waits for them, and re-layouts: 29.6 us -> none  [body(): terms.reshape(-1, block_size, block_size)]
    dot_general x1 -> x0, matrix products: 24.8 us -> none  [body(): jnp.einsum('eji,ekjl->ekil', p_blocks, hp_part, preferred_element_type=jn...]
    gather x1 -> x0, local copies, waits for them, and re-layouts: 22.8 us -> none  [body(): gathered = jnp.take(padded, lookup, axis=0)]
    convert_element_type x3 -> x0, other arithmetic: 22 us -> none  [the longest x1 17.3 us: body(): slab_part.astype(jnp.bfloat16)]
  transfers between devices with their start and end apart: 3 -> 3, of which waited for: 1 -> 0; matrix products, arithmetic and copies ran while one was open for 8% -> 1% of each run, Pallas kernels for 0% -> 20%
where the time goes in v1:
time: 78.3 us; the launch traced here: 78 us
  Pallas kernels  47.9 us (61%)
  blocking collectives  16.1 us (21%)
  starting transfers between devices  11 us (14%)
  local copies, waits for them, and re-layouts  2.19 us (3%)
  between operations  0.81 us (1%)
    pallas_call x1, Pallas kernels, galerkin(): pl.pallas_call(functools.partial(galerkin_kernel, n_agg), grid=(aggs,), i...  25.4 us
    pallas_call x2, Pallas kernels, paired(): pl.pallas_call(pair_kernel, grid=(count,), in_specs=[pl.BlockSpec((1, row...  17.4 us
    unnamed x1, blocking collectives  16.1 us
    ppermute x1, starting transfers between devices, body(): before = lax.ppermute(own[elems - face:], 'space', up)  5.57 us
    pallas_call x1, Pallas kernels, placed_rows(): pl.pallas_call(functools.partial(place_kernel, n_agg), in_specs=[pl.Block...  5.17 us
    all_to_all x1, starting transfers between devices, body(): lax.all_to_all(rows.reshape((n_agg, aggs // n_agg) + tail), 'agg', 0, 0)  4.16 us
    unnamed x15, local copies, waits for them, and re-layouts  2.15 us
  transfers between devices with their start and end apart: 3, of which 0 were waited for; matrix products, arithmetic and copies ran while one was open for 1% of the time, Pallas kernels for 20%

profile of v1, /device:TPU:0, one launch (start us, length us, event | category | flops | bytes accessed | tf_op | source)
XLA Modules:
  0.0 78.0 jit_solution(8308752450560631798)
XLA Ops:
  0.0 0.0 copy-start
  0.0 1.2 %copy-done = bf16[128,64,64]{0,2,1:T(8,128)(2,1)S(1)} copy-done((bf16[128,64,64]{0,2,1:T(8,128)(2,1)S(1)}, bf16[128,64,64]{0,2,1:T(8,128)(2,1)}, u32[]{:S(2)}) %copy-start) | copy-done | bytes 1048600
  1.2 1.9 %shard_map.65 = bf16[128,1,32,128]{3,2,1,0:T(8,128)(2,1)S(1)} custom-call(bf16[1,64,64,128]{3,2,1,0:T(8,128)(2,1)S(1)} %bitcast.20), custom_call_target="tpu_custom_call" | custom-call | bytes 2097152 | tf_op jit(solution)/shard_map/pallas_call | solution.py:27
  3.2 1.3 %collective-permute-start.1 = (bf16[32,32,128]{2,1,0:T(8,128)(2,1)S(1)}, bf16[32,32,128]{2,1,0:T(8,128)(2,1)S(1)}, u32[]{:S(2)}, u32[]{:S(2)}) collective-permute-start(bf16[32,32,128]{2,1,0:T(8,128)(2,1)S(1)} %get-tuple-element.5), channel_id=1, source_target_pairs={{8,0},{16,8},{24,16},{9,1},{17,9},{25,17},{10,2},{18,10},{26,18},{... | collective-permute-start | bytes 786440 | tf_op jit(solution)/shard_map/ppermute | solution.py:201
  4.5 5.6 %collective-permute-start = (bf16[32,32,128]{2,1,0:T(8,128)(2,1)S(1)}, bf16[32,32,128]{2,1,0:T(8,128)(2,1)S(1)}, u32[]{:S(2)}, u32[]{:S(2)}) collective-permute-start(bf16[32,32,128]{2,1,0:T(8,128)(2,1)S(1)} %get-tuple-element.6), channel_id=1, source_target_pairs={{0,8},{8,16},{16,24},{1,9},{9,17},{17,25},{2,10},{10,18},{18,26},{... | collective-permute-start | bytes 786440 | tf_op jit(solution)/shard_map/ppermute | solution.py:200
  10.0 0.0 copy-start.1
  10.1 0.0 copy-start.2
  10.1 0.0 copy-start.3
  10.1 0.0 copy-start.4
  10.1 15.5 %shard_map.64.h_ref = bf16[128,7,32,128]{3,2,1,0:T(8,128)(2,1)} custom-call(bf16[7,64,64,128]{3,2,1,0:T(8,128)(2,1)} %bitcast.23), custom_call_target="tpu_custom_call" | custom-call | bytes 14680064 | tf_op jit(solution)/shard_map/pallas_call | solution.py:27
  25.6 0.0 collective-permute-done.1.after_ref
  25.6 0.0 collective-permute-done.before_ref
  25.6 0.0 copy-done.1
  25.6 0.0 copy-done.2
  25.6 0.0 copy-done.3
  25.6 0.0 copy-done.4
  25.6 25.4 %shard_map.66 = bf16[16,4,64,128]{3,2,1,0:T(8,128)(2,1)} custom-call(s32[1]{0:T(128)} %bitcast.2.dev_ref, s32[7,128]{1,0:T(8,128)S(1)} %bitcast.21, s32[7,128]{1,0:T(8,128)S(1)} %bitcast.22, s32[128]{0:T(128)S(1)} %copy-done.3, s32[16]{0:T(128)S(1)} %copy-done.4, bf16[128,7,32,128]{3,2,1,0:T(8,128)(2,1)} %shard_map.64.h_ref, ...), custom_call_target="tpu_custom_call" | custom-call | tf_op jit(solution)/shard_map/pallas_call | solution.py:131
  51.0 4.2 %all-to-all-start = ((bf16[8,2,4,64,128]{4,3,2,1,0:T(8,128)(2,1)}), bf16[8,2,4,64,128]{4,3,2,1,0:T(8,128)(2,1)S(1)}, u32[]{:S(2)}, u32[]{:S(2)}) async-start(bf16[8,2,4,64,128]{4,3,2,1,0:T(8,128)(2,1)} %bitcast.12), calls=%async_computation | async-start | bytes 2097152 | tf_op jit(solution)/shard_map/all_to_all | solution.py:206
  55.1 0.0 copy-done.5
  55.2 0.7 dynamic-slice
  56.5 0.2 dynamic-update-slice
  56.7 16.1 %all-reduce.owner_ref = s32[128]{0:T(128)S(1)} all-reduce(s32[128]{0:T(128)S(1)} %dynamic-update-slice), channel_id=1, replica_groups=mesh['space'=4,'agg'=8] {'agg'}, use_global_device_ids=true, to_apply=%add | all-reduce | flops 128 | bytes 1024
  72.8 0.0 all-to-all-done
  72.8 5.2 %shard_map.67 = bf16[16,7,64,64]{3,2,1,0:T(8,128)(2,1)} custom-call(s32[1]{0:T(128)} %bitcast.me_ref, s32[128]{0:T(128)S(1)} %all-reduce.owner_ref, bf16[16,4,64,128]{3,2,1,0:T(8,128)(2,1)S(1)} %bitcast.19), custom_call_target="tpu_custom_call" | custom-call | tf_op jit(solution)/shard_map/pallas_call | solution.py:177
  (3 shorter events, 0.0 us)
Async XLA Ops:
  0.0 1.2 %copy-start = (bf16[128,64,64]{0,2,1:T(8,128)(2,1)S(1)}, bf16[128,64,64]{0,2,1:T(8,128)(2,1)}, u32[]{:S(2)}) copy-start(bf16[128,64,64]{0,2,1:T(8,128)(2,1)} %param.8) | copy-start | bytes 3145732
  3.2 22.4 %collective-permute-start.1 = (bf16[32,32,128]{2,1,0:T(8,128)(2,1)S(1)}, bf16[32,32,128]{2,1,0:T(8,128)(2,1)S(1)}, u32[]{:S(2)}, u32[]{:S(2)}) collective-permute-start(bf16[32,32,128]{2,1,0:T(8,128)(2,1)S(1)} %get-tuple-element.5), channel_id=1, source_target_pairs={{8,0},{16,8},{24,16},{9,1},{17,9},{25,17},{10,2},{18,10},{26,18},{... | collective-permute-start | bytes 786440 | tf_op jit(solution)/shard_map/ppermute | solution.py:201
  4.5 21.1 %collective-permute-start = (bf16[32,32,128]{2,1,0:T(8,128)(2,1)S(1)}, bf16[32,32,128]{2,1,0:T(8,128)(2,1)S(1)}, u32[]{:S(2)}, u32[]{:S(2)}) collective-permute-start(bf16[32,32,128]{2,1,0:T(8,128)(2,1)S(1)} %get-tuple-element.6), channel_id=1, source_target_pairs={{0,8},{8,16},{16,24},{1,9},{9,17},{17,25},{2,10},{10,18},{18,26},{... | collective-permute-start | bytes 786440 | tf_op jit(solution)/shard_map/ppermute | solution.py:200
  10.0 15.5 %copy-start.1 = (s32[128,7]{0,1:T(8,128)S(1)}, s32[128,7]{0,1:T(8,128)}, u32[]{:S(2)}) copy-start(s32[128,7]{0,1:T(8,128)} %param.7) | copy-start | bytes 10756
  10.1 15.5 %copy-start.2 = (s32[128,7]{0,1:T(8,128)S(1)}, s32[128,7]{0,1:T(8,128)}, u32[]{:S(2)}) copy-start(s32[128,7]{0,1:T(8,128)} %param.10) | copy-start | bytes 10756
  10.1 15.5 %copy-start.3 = (s32[128]{0:T(128)S(1)}, s32[128]{0:T(128)}, u32[]{:S(2)}) copy-start(s32[128]{0:T(128)} %agg_ref.1) | copy-start | bytes 1540
  10.1 15.5 %copy-start.4 = (s32[16]{0:T(128)S(1)}, s32[16]{0:T(128)}, u32[]{:S(2)}) copy-start(s32[16]{0:T(128)} %owner_ref.1) | copy-start | bytes 196
  25.6 29.6 %copy-start.5 = (u32[32]{0:T(128)S(1)}, u32[32]{0:T(128)}, u32[]{:S(2)}) copy-start(u32[32]{0:T(128)} %constant.13) | copy-start | bytes 388
  51.0 21.8 %all-to-all-start = ((bf16[8,2,4,64,128]{4,3,2,1,0:T(8,128)(2,1)}), bf16[8,2,4,64,128]{4,3,2,1,0:T(8,128)(2,1)S(1)}, u32[]{:S(2)}, u32[]{:S(2)}) async-start(bf16[8,2,4,64,128]{4,3,2,1,0:T(8,128)(2,1)} %bitcast.12), calls=%async_computation | async-start | bytes 2097152 | tf_op jit(solution)/shard_map/all_to_all | solution.py:206

commit v2 on v0

v2 whole, which is shorter than its diff:
```python
import functools

import jax
import jax.numpy as jnp
from jax import lax
from jax.experimental import pallas as pl
from jax.experimental.pallas import tpu as pltpu
from jax.sharding import PartitionSpec as P

KC = 7
VMEM_LIMIT = 24 * 1024 * 1024
PREPARE_VMEM = 52 * 1024 * 1024
PITCH = 8


def turn(blocks, store, turned):
    rows, _, elems = blocks.shape
    half = rows // 2
    pitch = elems + PITCH
    for q in range(half):
        both = jnp.concatenate([blocks[q], blocks[half + q]], axis=0)
        turned[pl.ds(q * pitch, elems), :] = both.T.astype(jnp.float32)
    for e in range(elems):
        store(e, turned[pl.ds(e, half, stride=pitch), :].astype(jnp.bfloat16))


def pair_kernel(x_ref, o_ref, turned):
    def store(e, block):
        o_ref[e] = block
    turn(x_ref, store, turned)


def paired(x):
    rows, cols, elems = x.shape
    half = rows // 2
    return pl.pallas_call(
        pair_kernel,
        in_specs=[pl.BlockSpec(memory_space=pltpu.VMEM)],
        out_specs=pl.BlockSpec(memory_space=pltpu.VMEM),
        out_shape=jax.ShapeDtypeStruct((elems, half, 2 * cols), x.dtype),
        scratch_shapes=[pltpu.VMEM((half * (elems + PITCH), 2 * cols), jnp.float32)],
        compiler_params=pltpu.CompilerParams(vmem_limit_bytes=VMEM_LIMIT),
    )(x)


def prepare_kernel(n_agg, agg_ref, owner_ref, h_ref, o_ref, order, within,
                   raw, turned, place, count, sems):
    for k in range(KC):
        pltpu.make_async_copy(h_ref.at[k], raw.at[k], sems.at[k]).start()
    elems = agg_ref.shape[0]
    aggs = owner_ref.shape[0]
    per_agg = elems // aggs
    cap = aggs // n_agg
    for i in range(aggs + n_agg):
        count[i] = 0

    def rank_row(r, c):
        spot = lax.rem(owner_ref[r], aggs * n_agg)
        owner = spot // aggs
        seen = count[aggs + owner]
        count[aggs + owner] = seen + 1
        spot_rank = owner * cap + seen
        place[r] = spot_rank * per_agg
        within[spot_rank] = spot - owner * aggs
        return c
    lax.fori_loop(0, aggs, rank_row, 0, unroll=4)

    def rank_elem(e, c):
        a = agg_ref[e]
        seen = place[a]
        place[a] = seen + 1
        order[seen] = e
        return c
    lax.fori_loop(0, elems, rank_elem, 0, unroll=8)

    def one(k, c):
        pltpu.make_async_copy(h_ref.at[k], raw.at[k], sems.at[k]).wait()

        def store(e, block):
            o_ref[e, k] = block
        turn(raw.at[k], store, turned)
        return c
    lax.fori_loop(0, KC, one, 0)


def prepare(n_agg, agg_map, owner_pos, x):
    count, rows, cols, elems = x.shape
    half = rows // 2
    aggs = owner_pos.shape[0]
    smem = pl.BlockSpec(memory_space=pltpu.SMEM)
    vmem = pl.BlockSpec(memory_space=pltpu.VMEM)
    return pl.pallas_call(
        functools.partial(prepare_kernel, n_agg),
        in_specs=[smem, smem, pl.BlockSpec(memory_space=pl.ANY)],
        out_specs=(vmem, smem, smem),
        out_shape=(
            jax.ShapeDtypeStruct((elems, count, half, 2 * cols), x.dtype),
            jax.ShapeDtypeStruct((elems,), jnp.int32),
            jax.ShapeDtypeStruct((aggs,), jnp.int32),
        ),
        scratch_shapes=[
            pltpu.VMEM(x.shape, x.dtype),
            pltpu.VMEM((half * (elems + PITCH), 2 * cols), jnp.float32),
            pltpu.SMEM((aggs,), jnp.int32),
            pltpu.SMEM((aggs + n_agg,), jnp.int32),
            pltpu.SemaphoreType.DMA((count,)),
        ],
        compiler_params=pltpu.CompilerParams(vmem_limit_bytes=PREPARE_VMEM),
        cost_estimate=pl.CostEstimate(flops=0, bytes_accessed=4 * x.size, transcendentals=0),
    )(agg_map, owner_pos, x)


def swap_halves(x):
    half = x.shape[-1] // 2
    return jnp.concatenate([x[:, half:], x[:, :half]], axis=1)


def galerkin_kernel(n_agg, dev_ref, cols_ref, slot_ref, order, within,
                    h_ref, before_ref, own_ref, after_ref, o_ref, dense, stack, total):
    elems = own_ref.shape[0]
    face = before_ref.shape[0]
    half, lanes = own_ref.shape[1:]
    size = lanes // 2
    groups = within.shape[0]
    per_agg = elems // groups
    low = lax.broadcasted_iota(jnp.int32, (half, lanes), 1) < size
    low2 = lax.broadcasted_iota(jnp.int32, (size, lanes), 1) < size

    def spread(src, first):
        def one(c, carry):
            x = src[c]
            y = swap_halves(x)
            zero = jnp.zeros_like(x)
            dense[first + c, 0:half] = jnp.where(low, x, zero)
            dense[first + c, half:2 * half] = jnp.where(low, y, zero)
            dense[first + c, 2 * half:3 * half] = jnp.where(low, zero, y)
            dense[first + c, 3 * half:4 * half] = jnp.where(low, zero, x)
            return carry
        lax.fori_loop(0, src.shape[0], one, 0, unroll=8)
    spread(before_ref, 0)
    spread(own_ref, face)
    spread(after_ref, face + elems)

    dev = dev_ref[0]
    base = dev * elems
    hop = n_agg * elems

    def group(g, carry):
        total[...] = jnp.zeros_like(total)
        for t in range(per_agg):
            e = order[g * per_agg + t]
            stack[pl.ds(t * half, half), :] = own_ref[e]
            for k in range(KC):
                x = cols_ref[k, e] - base
                c = jnp.where(x < 0, x + hop - (elems - face),
                              jnp.where(x >= elems, x - hop + face + elems, x + face))
                hp = jnp.dot(h_ref[e, k], dense[c], preferred_element_type=jnp.float32)
                total[slot_ref[k, e], pl.ds(t * half, half), :] += hp
        left = stack[...].T
        for j in range(0, KC, 2):
            if j + 1 < KC:
                right = jnp.concatenate([total[j], total[j + 1]], axis=1).astype(jnp.bfloat16)
            else:
                right = total[j].astype(jnp.bfloat16)
            r = jnp.dot(left, right, preferred_element_type=jnp.float32)
            a_top, a_bot = r[:size, :lanes], r[size:, :lanes]
            if j + 1 < KC:
                b_top, b_bot = r[:size, lanes:], r[size:, lanes:]
                out = jnp.where(low2, a_top, b_bot) + swap_halves(jnp.where(low2, b_top, a_bot))
            else:
                out = jnp.where(low2, a_top + swap_halves(a_bot), within[g].astype(jnp.float32))
            o_ref[g, j // 2] = out.astype(o_ref.dtype)
        return carry
    lax.fori_loop(0, groups, group, 0)


def galerkin(n_agg, dev, cols, slots, order, within, h, before, own, after):
    elems, _, half, lanes = h.shape
    face = before.shape[0]
    aggs = within.shape[0]
    smem = pl.BlockSpec(memory_space=pltpu.SMEM)
    vmem = pl.BlockSpec(memory_space=pltpu.VMEM)
    tiles = (KC + 1) // 2
    return pl.pallas_call(
        functools.partial(galerkin_kernel, n_agg),
        in_specs=[smem] * 5 + [vmem] * 4,
        out_specs=vmem,
        out_shape=jax.ShapeDtypeStruct((aggs, tiles, lanes // 2, lanes), jnp.bfloat16),
        scratch_shapes=[
            pltpu.VMEM((elems + 2 * face, lanes, lanes), jnp.bfloat16),
            pltpu.VMEM((elems // aggs * half, lanes), jnp.bfloat16),
            pltpu.VMEM((KC, elems // aggs * half, lanes), jnp.float32),
        ],
        compiler_params=pltpu.CompilerParams(vmem_limit_bytes=VMEM_LIMIT),
    )(dev, cols, slots, order, within, h, before, own, after)


def place_kernel(x_ref, o_ref, spots):
    rows, tiles, size, lanes = x_ref.shape
    high = lax.broadcasted_iota(jnp.int32, (16, lanes), 1) >= lanes // 2
    for s in range(rows):
        mark = jnp.where(high, x_ref[s, tiles - 1, 0:16].astype(jnp.float32), 0.0)
        spots[s] = jnp.max(mark).astype(jnp.int32)

    def row(s, carry):
        q = spots[s]
        for t in range(tiles):
            x = x_ref[s, t]
            o_ref[q, 2 * t] = x[:, :size]
            if 2 * t + 1 < KC:
                o_ref[q, 2 * t + 1] = x[:, size:]
        return carry
    lax.fori_loop(0, rows, row, 0, unroll=2)


def placed_rows(x):
    rows, tiles, size, lanes = x.shape
    return pl.pallas_call(
        place_kernel,
        in_specs=[pl.BlockSpec(memory_space=pltpu.VMEM)],
        out_specs=pl.BlockSpec(memory_space=pltpu.VMEM),
        out_shape=jax.ShapeDtypeStruct((rows, KC, size, size), x.dtype),
        scratch_shapes=[pltpu.SMEM((rows,), jnp.int32)],
        compiler_params=pltpu.CompilerParams(vmem_limit_bytes=VMEM_LIMIT),
    )(x)


def body(h_blocks, h_cols, p_blocks, agg_map, term_slot, owner_pos):
    elems = p_blocks.shape[0]
    face = elems // 4
    aggs = owner_pos.shape[0]
    n_agg = lax.axis_size("agg")
    n_space = lax.axis_size("space")
    device = lax.axis_index("space") * n_agg + lax.axis_index("agg")

    own = paired(p_blocks.transpose(1, 2, 0))
    up = [(i, i + 1) for i in range(n_space - 1)]
    down = [(j, i) for i, j in up]
    before = lax.ppermute(own[elems - face:], "space", up)
    after = lax.ppermute(own[:face], "space", down)
    h, order, within = prepare(n_agg, agg_map, owner_pos, h_blocks.transpose(1, 2, 3, 0))
    rows = galerkin(n_agg, device.reshape(1).astype(jnp.int32), h_cols.T, term_slot.T,
                    order, within, h, before, own, after)
    tail = rows.shape[1:]
    got = lax.all_to_all(rows.reshape((n_agg, aggs // n_agg) + tail), "agg", 0, 0)
    return placed_rows(got.reshape((aggs,) + tail))


def solution(mesh):
    placed = (
        P(("space", "agg"), None, None, None),
        P(("space", "agg"), None),
        P(("space", "agg"), None, None),
        P(("space", "agg")),
        P(("space", "agg"), None),
        P(("space", "agg")),
    )
    return jax.shard_map(
        body,
        mesh=mesh,
        in_specs=placed,
        out_specs=P(("space", "agg"), None, None, None),
        check_vma=False,
    )
```

time: 429 us -> 62.1 us (0.14)
  other arithmetic: 164 us -> 0 us
  waiting for transfers between devices: 106 us -> 0.01 us
  local copies, waits for them, and re-layouts: 111 us -> 5.65 us
  Pallas kernels: 0 us -> 29.9 us
  matrix products: 24.8 us -> 0 us
  blocking collectives: 0 us -> 19.3 us
  between operations: 13.5 us -> 0.11 us
    scatter-add x1 -> x0, other arithmetic: 137 us -> none  [body(): jax.ops.segment_sum(terms.reshape(-1, block_size, block_size), target, nu...]
    reduce_scatter x1 -> x0, waiting for transfers between devices: 106 us -> none  [body(): lax.psum_scatter(slab_part.astype(jnp.bfloat16), 'agg', scatter_dimension...]
    pallas_call x0 -> x4, Pallas kernels: none -> 29.9 us  [the longest x1 17.6 us: galerkin(): pl.pallas_call(functools.partial(galerkin_kernel, n_agg), in_specs=[smem]...]
    reshape x1 -> x0, local copies, waits for them, and re-layouts: 29.6 us -> none  [body(): terms.reshape(-1, block_size, block_size)]
    unnamed x9 -> x12, local copies, waits for them, and re-layouts: 33.6 us -> 5.61 us
    dot_general x1 -> x0, matrix products: 24.8 us -> none  [body(): jnp.einsum('eji,ekjl->ekil', p_blocks, hp_part, preferred_element_type=jn...]
    gather x1 -> x0, local copies, waits for them, and re-layouts: 22.8 us -> none  [body(): gathered = jnp.take(padded, lookup, axis=0)]
    convert_element_type x3 -> x0, other arithmetic: 22 us -> none  [the longest x1 17.3 us: body(): slab_part.astype(jnp.bfloat16)]
  transfers between devices with their start and end apart: 3 -> 2, of which waited for: 1 -> 0; matrix products, arithmetic and copies ran while one was open for 8% -> 0% of each run, Pallas kernels for 0% -> 15%
where the time goes in v2:
time: 62.1 us; the launch traced here: 61.8 us
  Pallas kernels  29.9 us (48%)
  blocking collectives  19.3 us (31%)
  starting transfers between devices  6.86 us (11%)
  local copies, waits for them, and re-layouts  5.65 us (9%)
    all_to_all x1, blocking collectives, body(): lax.all_to_all(rows.reshape((n_agg, aggs // n_agg) + tail), 'agg', 0, 0)  19.3 us
    pallas_call x1, Pallas kernels, galerkin(): pl.pallas_call(functools.partial(galerkin_kernel, n_agg), in_specs=[smem]...  17.6 us
    pallas_call x1, Pallas kernels, prepare(): pl.pallas_call(functools.partial(prepare_kernel, n_agg), in_specs=[smem,...  9.32 us
    unnamed x12, local copies, waits for them, and re-layouts  5.61 us
    ppermute x1, starting transfers between devices, body(): before = lax.ppermute(own[elems - face:], 'space', up)  5.57 us
    pallas_call x1, Pallas kernels, placed_rows(): pl.pallas_call(place_kernel, in_specs=[pl.BlockSpec(memory_space=pltpu.VM...  2.32 us
    ppermute x1, starting transfers between devices, body(): after = lax.ppermute(own[:face], 'space', down)  1.29 us
  transfers between devices with their start and end apart: 2, of which 0 were waited for; matrix products, arithmetic and copies ran while one was open for 0% of the time, Pallas kernels for 15%

profile of v2, /device:TPU:0, one launch (start us, length us, event | category | flops | bytes accessed | tf_op | source)
XLA Modules:
  0.0 61.8 jit_solution(5185780288098010498)
XLA Ops:
  0.0 0.0 copy-start.1
  0.0 1.2 %copy-done.1 = bf16[128,64,64]{0,2,1:T(8,128)(2,1)S(1)} copy-done((bf16[128,64,64]{0,2,1:T(8,128)(2,1)S(1)}, bf16[128,64,64]{0,2,1:T(8,128)(2,1)}, u32[]{:S(2)}) %copy-start.1) | copy-done | bytes 1048600
  1.2 0.0 copy-start.2
  1.2 0.0 copy-start.3
  1.2 0.6 %shard_map.65.own_ref = bf16[128,32,128]{2,1,0:T(8,128)(2,1)S(1)} custom-call(bf16[64,64,128]{2,1,0:T(8,128)(2,1)S(1)} %bitcast.9), custom_call_target="tpu_custom_call" | custom-call | tf_op jit(solution)/shard_map/pallas_call | solution.py:36
  1.9 1.3 %collective-permute-start.1 = (bf16[32,32,128]{2,1,0:T(8,128)(2,1)S(1)}, bf16[32,32,128]{2,1,0:T(8,128)(2,1)S(1)}, u32[]{:S(2)}, u32[]{:S(2)}) collective-permute-start(bf16[32,32,128]{2,1,0:T(8,128)(2,1)S(1)} %get-tuple-element.11), channel_id=1, source_target_pairs={{8,0},{16,8},{24,16},{9,1},{17,9},{25,17},{10,2},{18,10},{26,18},{... | collective-permute-start | bytes 786440 | tf_op jit(solution)/shard_map/ppermute | solution.py:240
  3.2 5.6 %collective-permute-start = (bf16[32,32,128]{2,1,0:T(8,128)(2,1)S(1)}, bf16[32,32,128]{2,1,0:T(8,128)(2,1)S(1)}, u32[]{:S(2)}, u32[]{:S(2)}) collective-permute-start(bf16[32,32,128]{2,1,0:T(8,128)(2,1)S(1)} %get-tuple-element.12), channel_id=1, source_target_pairs={{0,8},{8,16},{16,24},{1,9},{9,17},{17,25},{2,10},{10,18},{18,26},{... | collective-permute-start | bytes 786440 | tf_op jit(solution)/shard_map/ppermute | solution.py:239
  8.8 0.0 copy-start.4
  8.8 0.6 %copy-done.4 = s32[128]{0:T(128)S(1)} copy-done((s32[128]{0:T(128)S(1)}, s32[128]{0:T(128)}, u32[]{:S(2)}) %copy-start.4) | copy-done | bytes 536
  9.5 0.0 copy-start.5
  9.5 0.7 %copy-done.5 = s32[16]{0:T(128)S(1)} copy-done((s32[16]{0:T(128)S(1)}, s32[16]{0:T(128)}, u32[]{:S(2)}) %copy-start.5) | copy-done | bytes 88
  10.1 9.3 %shard_map.64 = (bf16[128,7,32,128]{3,2,1,0:T(8,128)(2,1)}, s32[128]{0:T(128)S(1)}, s32[16]{0:T(128)S(1)}) custom-call(s32[128]{0:T(128)S(1)} %copy-done.4, s32[16]{0:T(128)S(1)} %copy-done.5, bf16[7,64,64,128]{3,2,1,0:T(8,128)(2,1)} %bitcast.12), custom_call_target="tpu_custom_call" | custom-call | bytes 14680064 | tf_op jit(solution)/shard_map/pallas_call | solution.py:92
  19.5 0.0 collective-permute-done.1.after_ref
  19.5 0.0 collective-permute-done.before_ref
  19.5 0.0 copy-done.2
  19.5 0.0 copy-done.3
  19.5 0.0 copy-start
  19.5 3.1 %copy-done = bf16[128,7,32,128]{3,2,1,0:T(8,128)(2,1)S(1)} copy-done((bf16[128,7,32,128]{3,2,1,0:T(8,128)(2,1)S(1)}, bf16[128,7,32,128]{3,2,1,0:T(8,128)(2,1)}, u32[]{:S(2)}) %copy-start) | copy-done | bytes 7340056
  22.6 17.6 %shard_map.66 = bf16[16,4,64,128]{3,2,1,0:T(8,128)(2,1)S(1)} custom-call(s32[1]{0:T(128)} %bitcast.dev_ref, s32[7,128]{1,0:T(8,128)S(1)} %bitcast.10, s32[7,128]{1,0:T(8,128)S(1)} %bitcast.11, s32[128]{0:T(128)S(1)} %get-tuple-element.8.order, s32[16]{0:T(128)S(1)} %get-tuple-element.9.within, bf16[128,7,32,128]{3,2,1,0:T(8,128)(2,1)S(1)} %copy-done, ...), custom_call_target="tpu_custom_call" | custom-call | tf_op jit(solution)/shard_map/pallas_call | solution.py:184
  40.2 19.3 %all_to_all.5 = bf16[8,2,4,64,128]{4,3,2,1,0:T(8,128)(2,1)S(1)} all-to-all(bf16[8,2,4,64,128]{4,3,2,1,0:T(8,128)(2,1)S(1)} %bitcast.7), channel_id=1, replica_groups=mesh['space'=4,'agg'=8] {'agg'}, dimensions={0} | all-to-all | bytes 2097152 | tf_op jit(solution)/shard_map/all_to_all | solution.py:245
  59.5 2.3 %shard_map.67 = bf16[16,7,64,64]{3,2,1,0:T(8,128)(2,1)} custom-call(bf16[16,4,64,128]{3,2,1,0:T(8,128)(2,1)S(1)} %bitcast.8), custom_call_target="tpu_custom_call" | custom-call | tf_op jit(solution)/shard_map/pallas_call | solution.py:218
  (1 shorter events, 0.0 us)
Async XLA Ops:
  0.0 1.2 %copy-start.1 = (bf16[128,64,64]{0,2,1:T(8,128)(2,1)S(1)}, bf16[128,64,64]{0,2,1:T(8,128)(2,1)}, u32[]{:S(2)}) copy-start(bf16[128,64,64]{0,2,1:T(8,128)(2,1)} %param.8) | copy-start | bytes 3145732
  1.2 18.3 %copy-start.2 = (s32[128,7]{0,1:T(8,128)S(1)}, s32[128,7]{0,1:T(8,128)}, u32[]{:S(2)}) copy-start(s32[128,7]{0,1:T(8,128)} %param.7) | copy-start | bytes 10756
  1.2 18.3 %copy-start.3 = (s32[128,7]{0,1:T(8,128)S(1)}, s32[128,7]{0,1:T(8,128)}, u32[]{:S(2)}) copy-start(s32[128,7]{0,1:T(8,128)} %param.10) | copy-start | bytes 10756
  1.9 17.5 %collective-permute-start.1 = (bf16[32,32,128]{2,1,0:T(8,128)(2,1)S(1)}, bf16[32,32,128]{2,1,0:T(8,128)(2,1)S(1)}, u32[]{:S(2)}, u32[]{:S(2)}) collective-permute-start(bf16[32,32,128]{2,1,0:T(8,128)(2,1)S(1)} %get-tuple-element.11), channel_id=1, source_target_pairs={{8,0},{16,8},{24,16},{9,1},{17,9},{25,17},{10,2},{18,10},{26,18},{... | collective-permute-start | bytes 786440 | tf_op jit(solution)/shard_map/ppermute | solution.py:240
  3.2 16.2 %collective-permute-start = (bf16[32,32,128]{2,1,0:T(8,128)(2,1)S(1)}, bf16[32,32,128]{2,1,0:T(8,128)(2,1)S(1)}, u32[]{:S(2)}, u32[]{:S(2)}) collective-permute-start(bf16[32,32,128]{2,1,0:T(8,128)(2,1)S(1)} %get-tuple-element.12), channel_id=1, source_target_pairs={{0,8},{8,16},{16,24},{1,9},{9,17},{17,25},{2,10},{10,18},{18,26},{... | collective-permute-start | bytes 786440 | tf_op jit(solution)/shard_map/ppermute | solution.py:239
  8.8 0.7 %copy-start.4 = (s32[128]{0:T(128)S(1)}, s32[128]{0:T(128)}, u32[]{:S(2)}) copy-start(s32[128]{0:T(128)} %agg_ref.1) | copy-start | bytes 1540
  9.5 0.7 %copy-start.5 = (s32[16]{0:T(128)S(1)}, s32[16]{0:T(128)}, u32[]{:S(2)}) copy-start(s32[16]{0:T(128)} %owner_ref.1) | copy-start | bytes 196
  19.5 3.1 %copy-start = (bf16[128,7,32,128]{3,2,1,0:T(8,128)(2,1)S(1)}, bf16[128,7,32,128]{3,2,1,0:T(8,128)(2,1)}, u32[]{:S(2)}) copy-start(bf16[128,7,32,128]{3,2,1,0:T(8,128)(2,1)} %get-tuple-element.10.h_ref) | copy-start | bytes 22020100

commit v3 on v2

--- a/solution.py
+++ b/solution.py
@@ -9,7 +9,7 @@
 
 KC = 7
 VMEM_LIMIT = 24 * 1024 * 1024
-PREPARE_VMEM = 52 * 1024 * 1024
+PREPARE_VMEM = 45 * 1024 * 1024
 PITCH = 8
 
 
@@ -24,44 +24,24 @@
         store(e, turned[pl.ds(e, half, stride=pitch), :].astype(jnp.bfloat16))
 
 
-def pair_kernel(x_ref, o_ref, turned):
-    def store(e, block):
-        o_ref[e] = block
-    turn(x_ref, store, turned)
-
-
-def paired(x):
-    rows, cols, elems = x.shape
-    half = rows // 2
-    return pl.pallas_call(
-        pair_kernel,
-        in_specs=[pl.BlockSpec(memory_space=pltpu.VMEM)],
-        out_specs=pl.BlockSpec(memory_space=pltpu.VMEM),
-        out_shape=jax.ShapeDtypeStruct((elems, half, 2 * cols), x.dtype),
-        scratch_shapes=[pltpu.VMEM((half * (elems + PITCH), 2 * cols), jnp.float32)],
-        compiler_params=pltpu.CompilerParams(vmem_limit_bytes=VMEM_LIMIT),
-    )(x)
-
-
-def prepare_kernel(n_agg, agg_ref, owner_ref, h_ref, o_ref, order, within,
-                   raw, turned, place, count, sems):
-    for k in range(KC):
-        pltpu.make_async_copy(h_ref.at[k], raw.at[k], sems.at[k]).start()
+def sort_and_pair_kernel(n_agg, agg_ref, owner_ref, p_ref, o_ref, order, within,
+                         raw, turned, place, count, sem):
+    copy = pltpu.make_async_copy(p_ref, raw, sem)
+    copy.start()
     elems = agg_ref.shape[0]
     aggs = owner_ref.shape[0]
     per_agg = elems // aggs
     cap = aggs // n_agg
-    for i in range(aggs + n_agg):
-        count[i] = 0
+    for i in range(n_agg):
+        count[i] = i * cap
 
     def rank_row(r, c):
         spot = lax.rem(owner_ref[r], aggs * n_agg)
         owner = spot // aggs
-        seen = count[aggs + owner]
-        count[aggs + owner] = seen + 1
-        spot_rank = owner * cap + seen
-        place[r] = spot_rank * per_agg
-        within[spot_rank] = spot - owner * aggs
+        rank = count[owner]
+        count[owner] = rank + 1
+        place[r] = rank * per_agg
+        within[rank] = spot - owner * aggs
         return c
     lax.fori_loop(0, aggs, rank_row, 0, unroll=4)
 
@@ -72,29 +52,25 @@
         order[seen] = e
         return c
     lax.fori_loop(0, elems, rank_elem, 0, unroll=8)
-
-    def one(k, c):
-        pltpu.make_async_copy(h_ref.at[k], raw.at[k], sems.at[k]).wait()
-
-        def store(e, block):
-            o_ref[e, k] = block
-        turn(raw.at[k], store, turned)
-        return c
-    lax.fori_loop(0, KC, one, 0)
-
-
-def prepare(n_agg, agg_map, owner_pos, x):
-    count, rows, cols, elems = x.shape
+    copy.wait()
+
+    def store(e, block):
+        o_ref[e] = block
+    turn(raw, store, turned)
+
+
+def sort_and_pair(n_agg, agg_map, owner_pos, x):
+    rows, cols, elems = x.shape
     half = rows // 2
     aggs = owner_pos.shape[0]
     smem = pl.BlockSpec(memory_space=pltpu.SMEM)
     vmem = pl.BlockSpec(memory_space=pltpu.VMEM)
     return pl.pallas_call(
-        functools.partial(prepare_kernel, n_agg),
+        functools.partial(sort_and_pair_kernel, n_agg),
         in_specs=[smem, smem, pl.BlockSpec(memory_space=pl.ANY)],
         out_specs=(vmem, smem, smem),
         out_shape=(
-            jax.ShapeDtypeStruct((elems, count, half, 2 * cols), x.dtype),
+            jax.ShapeDtypeStruct((elems, half, 2 * cols), x.dtype),
             jax.ShapeDtypeStruct((elems,), jnp.int32),
             jax.ShapeDtypeStruct((aggs,), jnp.int32),
         ),
@@ -102,12 +78,147 @@
             pltpu.VMEM(x.shape, x.dtype),
             pltpu.VMEM((half * (elems + PITCH), 2 * cols), jnp.float32),
             pltpu.SMEM((aggs,), jnp.int32),
-            pltpu.SMEM((aggs + n_agg,), jnp.int32),
-            pltpu.SemaphoreType.DMA((count,)),
+            pltpu.SMEM((n_agg,), jnp.int32),
+            pltpu.SemaphoreType.DMA,
         ],
         compiler_params=pltpu.CompilerParams(vmem_limit_bytes=PREPARE_VMEM),
-        cost_estimate=pl.CostEstimate(flops=0, bytes_accessed=4 * x.size, transcendentals=0),
     )(agg_map, owner_pos, x)
+
+
+def prepare_kernel(h_ref, own_ref, o_ref, before_ref, after_ref,
+                   raw, turned, sems, up_sems, down_sems):
+    for k in range(KC):
+        pltpu.make_async_copy(h_ref.at[k], raw.at[k], sems.at[k]).start()
+    slab = lax.axis_index("space")
+    slabs = lax.axis_size("space")
+    elems = own_ref.shape[0]
+    face = before_ref.shape[0]
+    lower, upper = slab > 0, slab < slabs - 1
+    barrier = pltpu.get_barrier_semaphore()
+
+    def upward():
+        return pltpu.make_async_remote_copy(
+            src_ref=own_ref.at[pl.ds(elems - face, face)], dst_ref=before_ref,
+            send_sem=up_sems.at[0], recv_sem=up_sems.at[1],
+            device_id={"space": slab + 1}, device_id_type=pl.DeviceIdType.MESH)
+
+    def downward():
+        return pltpu.make_async_remote_copy(
+            src_ref=own_ref.at[pl.ds(0, face)], dst_ref=after_ref,
+            send_sem=down_sems.at[0], recv_sem=down_sems.at[1],
+            device_id={"space": slab - 1}, device_id_type=pl.DeviceIdType.MESH)
+
+    @pl.when(upper)
+    def _():
+        pl.semaphore_signal(barrier, inc=1, device_id={"space": slab + 1},
+                            device_id_type=pl.DeviceIdType.MESH)
+
+    @pl.when(lower)
+    def _():
+        pl.semaphore_signal(barrier, inc=1, device_id={"space": slab - 1},
+                            device_id_type=pl.DeviceIdType.MESH)
+
+    def one(k, c):
+        pltpu.make_async_copy(h_ref.at[k], raw.at[k], sems.at[k]).wait()
+
+        def store(e, block):
+            o_ref[e, k] = block
+        turn(raw.at[k], store, turned)
+        return c
+    lax.fori_loop(0, 1, one, 0)
+    pl.semaphore_wait(barrier, lower.astype(jnp.int32) + upper.astype(jnp.int32))
+
+    @pl.when(upper)
+    def _():
+        upward().start()
+
+    @pl.when(lower)
+    def _():
+        downward().start()
+    lax.fori_loop(1, KC, one, 0)
+
+    @pl.when(upper)
+    def _():
+        upward().wait_send()
+        downward().wait_recv()
+
+    @pl.when(lower)
+    def _():
+        downward().wait_send()
+        upward().wait_recv()
+
+    @pl.when(jnp.logical_not(upper))
+    def _():
+        after_ref[...] = jnp.zeros_like(after_ref)
+
+    @pl.when(jnp.logical_not(lower))
+    def _():
+        before_ref[...] = jnp.zeros_like(before_ref)
+
+
+def prepare(x, own):
+    count, rows, cols, elems = x.shape
+    half = rows // 2
+    face = elems // 4
+    vmem = pl.BlockSpec(memory_space=pltpu.VMEM)
+    edge = jax.ShapeDtypeStruct((face, half, 2 * cols), x.dtype)
+    return pl.pallas_call(
+        prepare_kernel,
+        in_specs=[pl.BlockSpec(memory_space=pl.ANY), vmem],
+        out_specs=(vmem, vmem, vmem),
+        out_shape=(jax.ShapeDtypeStruct((elems, count, half, 2 * cols), x.dtype), edge, edge),
+        scratch_shapes=[
+            pltpu.VMEM(x.shape, x.dtype),
+            pltpu.VMEM((half * (elems + PITCH), 2 * cols), jnp.float32),
+            pltpu.SemaphoreType.DMA((count,)),
+            pltpu.SemaphoreType.DMA((2,)),
+            pltpu.SemaphoreType.DMA((2,)),
+        ],
+        compiler_params=pltpu.CompilerParams(
+            vmem_limit_bytes=PREPARE_VMEM, collective_id=0, has_side_effects=True),
+    )(x, own)
+
+
+def exchange_kernel(n_agg, x_ref, o_ref, send_sems, recv_sems, local_sem):
+    cap = x_ref.shape[0] // n_agg
+    me = lax.axis_index("agg")
+    barrier = pltpu.get_barrier_semaphore()
+    for d in range(1, n_agg):
+        pl.semaphore_signal(barrier, inc=1, device_id={"agg": lax.rem(me + d, n_agg)},
+                            device_id_type=pl.DeviceIdType.MESH)
+    mine = pl.ds(me * cap, cap)
+    local = pltpu.make_async_copy(x_ref.at[mine], o_ref.at[mine], local_sem)
+    local.start()
+    pl.semaphore_wait(barrier, n_agg - 1)
+    copies = []
+    for d in range(1, n_agg):
+        peer = lax.rem(me + d, n_agg)
+        copy = pltpu.make_async_remote_copy(
+            src_ref=x_ref.at[pl.ds(peer * cap, cap)], dst_ref=o_ref.at[mine],
+            send_sem=send_sems.at[d], recv_sem=recv_sems.at[d],
+            device_id={"agg": peer}, device_id_type=pl.DeviceIdType.MESH)
+        copy.start()
+        copies.append(copy)
+    local.wait()
+    for copy in copies:
+        copy.wait()
+
+
+def exchanged(n_agg, x):
+    vmem = pl.BlockSpec(memory_space=pltpu.VMEM)
+    return pl.pallas_call(
+        functools.partial(exchange_kernel, n_agg),
+        in_specs=[vmem],
+        out_specs=vmem,
+        out_shape=jax.ShapeDtypeStruct(x.shape, x.dtype),
+        scratch_shapes=[
+            pltpu.SemaphoreType.DMA((n_agg,)),
+            pltpu.SemaphoreType.DMA((n_agg,)),
+            pltpu.SemaphoreType.DMA,
+        ],
+        compiler_params=pltpu.CompilerParams(
+            vmem_limit_bytes=VMEM_LIMIT, collective_id=1, has_side_effects=True),
+    )(x)
 
 
 def swap_halves(x):
@@ -226,24 +337,13 @@
 
 
 def body(h_blocks, h_cols, p_blocks, agg_map, term_slot, owner_pos):
-    elems = p_blocks.shape[0]
-    face = elems // 4
-    aggs = owner_pos.shape[0]
     n_agg = lax.axis_size("agg")
-    n_space = lax.axis_size("space")
     device = lax.axis_index("space") * n_agg + lax.axis_index("agg")
-
-    own = paired(p_blocks.transpose(1, 2, 0))
-    up = [(i, i + 1) for i in range(n_space - 1)]
-    down = [(j, i) for i, j in up]
-    before = lax.ppermute(own[elems - face:], "space", up)
-    after = lax.ppermute(own[:face], "space", down)
-    h, order, within = prepare(n_agg, agg_map, owner_pos, h_blocks.transpose(1, 2, 3, 0))
+    own, order, within = sort_and_pair(n_agg, agg_map, owner_pos, p_blocks.transpose(1, 2, 0))
+    h, before, after = prepare(h_blocks.transpose(1, 2, 3, 0), own)
     rows = galerkin(n_agg, device.reshape(1).astype(jnp.int32), h_cols.T, term_slot.T,
                     order, within, h, before, own, after)
-    tail = rows.shape[1:]
-    got = lax.all_to_all(rows.reshape((n_agg, aggs // n_agg) + tail), "agg", 0, 0)
-    return placed_rows(got.reshape((aggs,) + tail))
+    return placed_rows(exchanged(n_agg, rows))
 
 
 def solution(mesh):

time: 62.1 us -> 51 us (0.82)
  blocking collectives: 19.3 us -> 0 us
  Pallas kernels: 29.9 us -> 47.8 us
  starting transfers between devices: 6.86 us -> 0 us
  local copies, waits for them, and re-layouts: 5.65 us -> 2.57 us
    all_to_all x1 -> x0, blocking collectives: 19.3 us -> none  [body(): lax.all_to_all(rows.reshape((n_agg, aggs // n_agg) + tail), 'agg', 0, 0)]
    pallas_call x2 -> x3, Pallas kernels: 9.97 us -> 27.9 us  [the longest x1 14.4 us: exchanged(): pl.pallas_call(functools.partial(exchange_kernel, n_agg), in_specs=[vmem]...]
    ppermute x2 -> x0, starting transfers between devices: 6.86 us -> none  [the longest x1 5.57 us: body(): before = lax.ppermute(own[elems - face:], 'space', up)]
    unnamed x12 -> x10, local copies, waits for them, and re-layouts: 5.61 us -> 2.57 us
  transfers between devices with their start and end apart: 2 -> 0, of which waited for: 0 -> 0; matrix products, arithmetic and copies ran while one was open for 0% -> 0% of each run, Pallas kernels for 15% -> 0%
where the time goes in v3:
time: 51 us; the launch traced here: 50.4 us
  Pallas kernels  47.8 us (94%)
  local copies, waits for them, and re-layouts  2.57 us (5%)
    pallas_call x1, Pallas kernels, galerkin(): pl.pallas_call(functools.partial(galerkin_kernel, n_agg), in_specs=[smem]...  17.6 us
    pallas_call x1, Pallas kernels, exchanged(): pl.pallas_call(functools.partial(exchange_kernel, n_agg), in_specs=[vmem]...  14.4 us
    pallas_call x1, Pallas kernels, prepare(): pl.pallas_call(prepare_kernel, in_specs=[pl.BlockSpec(memory_space=pl.ANY...  11.3 us
    unnamed x10, local copies, waits for them, and re-layouts  2.57 us
    pallas_call x1, Pallas kernels, placed_rows(): pl.pallas_call(place_kernel, in_specs=[pl.BlockSpec(memory_space=pltpu.VM...  2.32 us
    pallas_call x1, Pallas kernels, sort_and_pair(): pl.pallas_call(functools.partial(sort_and_pair_kernel, n_agg), in_specs=[...  2.11 us

profile of v3, /device:TPU:0, one launch (start us, length us, event | category | flops | bytes accessed | tf_op | source)
XLA Modules:
  0.0 50.4 jit_solution(3421053815225911616)
XLA Ops:
  0.0 0.0 copy-start.2
  0.0 0.0 copy-start.1
  0.0 0.0 copy-start
  0.0 1.2 %copy-done = bf16[128,64,64]{0,2,1:T(8,128)(2,1)S(1)} copy-done((bf16[128,64,64]{0,2,1:T(8,128)(2,1)S(1)}, bf16[128,64,64]{0,2,1:T(8,128)(2,1)}, u32[]{:S(2)}) %copy-start) | copy-done | bytes 1048600
  1.3 0.0 copy-start.3
  1.3 0.7 %copy-done.3 = s32[128]{0:T(128)S(1)} copy-done((s32[128]{0:T(128)S(1)}, s32[128]{0:T(128)}, u32[]{:S(2)}) %copy-start.3) | copy-done | bytes 536
  1.9 0.0 copy-start.4
  1.9 0.7 %copy-done.4 = s32[16]{0:T(128)S(1)} copy-done((s32[16]{0:T(128)S(1)}, s32[16]{0:T(128)}, u32[]{:S(2)}) %copy-start.4) | copy-done | bytes 88
  2.6 2.1 %shard_map.64 = (bf16[128,32,128]{2,1,0:T(8,128)(2,1)S(1)}, s32[128]{0:T(128)S(1)}, s32[16]{0:T(128)S(1)}) custom-call(s32[128]{0:T(128)S(1)} %copy-done.3, s32[16]{0:T(128)S(1)} %copy-done.4, bf16[64,64,128]{2,1,0:T(8,128)(2,1)S(1)} %bitcast.5), custom_call_target="tpu_custom_call" | custom-call | tf_op jit(solution)/shard_map/pallas_call | solution.py:68
  4.7 11.3 %shard_map.65 = (bf16[128,7,32,128]{3,2,1,0:T(8,128)(2,1)S(1)}, bf16[32,32,128]{2,1,0:T(8,128)(2,1)S(1)}, bf16[32,32,128]{2,1,0:T(8,128)(2,1)S(1)}) custom-call(bf16[7,64,64,128]{3,2,1,0:T(8,128)(2,1)} %bitcast.8, bf16[128,32,128]{2,1,0:T(8,128)(2,1)S(1)} %get-tuple-element.13.own_ref), custom_call_target="tpu_custom_call" | custom-call | tf_op jit(solution)/shard_map/pallas_call | solution.py:165
  16.0 0.0 copy-done.2
  16.0 0.0 copy-done.1
  16.1 17.6 %shard_map.66.x_ref = bf16[16,4,64,128]{3,2,1,0:T(8,128)(2,1)S(1)} custom-call(s32[1]{0:T(128)} %bitcast.dev_ref, s32[7,128]{1,0:T(8,128)S(1)} %bitcast.6, s32[7,128]{1,0:T(8,128)S(1)} %bitcast.7, s32[128]{0:T(128)S(1)} %get-tuple-element.11.order, s32[16]{0:T(128)S(1)} %get-tuple-element.12.within, bf16[128,7,32,128]{3,2,1,0:T(8,128)(2,1)S(1)} %get-tuple-element.14.h_ref, ...), custom_call_target="tpu_custom_call" | custom-call | tf_op jit(solution)/shard_map/pallas_call | solution.py:295
  33.7 14.4 %shard_map.67.x_ref = bf16[16,4,64,128]{3,2,1,0:T(8,128)(2,1)S(1)} custom-call(bf16[16,4,64,128]{3,2,1,0:T(8,128)(2,1)S(1)} %shard_map.66.x_ref), custom_call_target="tpu_custom_call" | custom-call | tf_op jit(solution)/shard_map/pallas_call | solution.py:209
  48.1 2.3 %shard_map.68 = bf16[16,7,64,64]{3,2,1,0:T(8,128)(2,1)} custom-call(bf16[16,4,64,128]{3,2,1,0:T(8,128)(2,1)S(1)} %shard_map.67.x_ref), custom_call_target="tpu_custom_call" | custom-call | tf_op jit(solution)/shard_map/pallas_call | solution.py:329
Async XLA Ops:
  0.0 16.0 %copy-start.2 = (s32[128,7]{0,1:T(8,128)S(1)}, s32[128,7]{0,1:T(8,128)}, u32[]{:S(2)}) copy-start(s32[128,7]{0,1:T(8,128)} %param.10) | copy-start | bytes 10756
  0.0 16.0 %copy-start.1 = (s32[128,7]{0,1:T(8,128)S(1)}, s32[128,7]{0,1:T(8,128)}, u32[]{:S(2)}) copy-start(s32[128,7]{0,1:T(8,128)} %param.7) | copy-start | bytes 10756
  0.0 1.3 %copy-start = (bf16[128,64,64]{0,2,1:T(8,128)(2,1)S(1)}, bf16[128,64,64]{0,2,1:T(8,128)(2,1)}, u32[]{:S(2)}) copy-start(bf16[128,64,64]{0,2,1:T(8,128)(2,1)} %param.8) | copy-start | bytes 3145732
  1.3 0.7 %copy-start.3 = (s32[128]{0:T(128)S(1)}, s32[128]{0:T(128)}, u32[]{:S(2)}) copy-start(s32[128]{0:T(128)} %agg_ref.1) | copy-start | bytes 1540
  1.9 0.7 %copy-start.4 = (s32[16]{0:T(128)S(1)}, s32[16]{0:T(128)}, u32[]{:S(2)}) copy-start(s32[16]{0:T(128)} %owner_ref.1) | copy-start | bytes 196

commit v4 on v3

--- a/solution.py
+++ b/solution.py
@@ -179,61 +179,26 @@
     )(x, own)
 
 
-def exchange_kernel(n_agg, x_ref, o_ref, send_sems, recv_sems, local_sem):
-    cap = x_ref.shape[0] // n_agg
-    me = lax.axis_index("agg")
-    barrier = pltpu.get_barrier_semaphore()
-    for d in range(1, n_agg):
-        pl.semaphore_signal(barrier, inc=1, device_id={"agg": lax.rem(me + d, n_agg)},
-                            device_id_type=pl.DeviceIdType.MESH)
-    mine = pl.ds(me * cap, cap)
-    local = pltpu.make_async_copy(x_ref.at[mine], o_ref.at[mine], local_sem)
-    local.start()
-    pl.semaphore_wait(barrier, n_agg - 1)
-    copies = []
-    for d in range(1, n_agg):
-        peer = lax.rem(me + d, n_agg)
-        copy = pltpu.make_async_remote_copy(
-            src_ref=x_ref.at[pl.ds(peer * cap, cap)], dst_ref=o_ref.at[mine],
-            send_sem=send_sems.at[d], recv_sem=recv_sems.at[d],
-            device_id={"agg": peer}, device_id_type=pl.DeviceIdType.MESH)
-        copy.start()
-        copies.append(copy)
-    local.wait()
-    for copy in copies:
-        copy.wait()
-
-
-def exchanged(n_agg, x):
-    vmem = pl.BlockSpec(memory_space=pltpu.VMEM)
-    return pl.pallas_call(
-        functools.partial(exchange_kernel, n_agg),
-        in_specs=[vmem],
-        out_specs=vmem,
-        out_shape=jax.ShapeDtypeStruct(x.shape, x.dtype),
-        scratch_shapes=[
-            pltpu.SemaphoreType.DMA((n_agg,)),
-            pltpu.SemaphoreType.DMA((n_agg,)),
-            pltpu.SemaphoreType.DMA,
-        ],
-        compiler_params=pltpu.CompilerParams(
-            vmem_limit_bytes=VMEM_LIMIT, collective_id=1, has_side_effects=True),
-    )(x)
-
-
 def swap_halves(x):
     half = x.shape[-1] // 2
     return jnp.concatenate([x[:, half:], x[:, :half]], axis=1)
 
 
 def galerkin_kernel(n_agg, dev_ref, cols_ref, slot_ref, order, within,
-                    h_ref, before_ref, own_ref, after_ref, o_ref, dense, stack, total):
+                    h_ref, before_ref, own_ref, after_ref, o_ref,
+                    dense, stack, sums, rows, send_sems, recv_sems):
     elems = own_ref.shape[0]
     face = before_ref.shape[0]
     half, lanes = own_ref.shape[1:]
     size = lanes // 2
     groups = within.shape[0]
     per_agg = elems // groups
+    cap = groups // n_agg
+    me = lax.axis_index("agg")
+    mesh_id = pl.DeviceIdType.MESH
+    barrier = pltpu.get_barrier_semaphore()
+    for d in range(1, n_agg):
+        pl.semaphore_signal(barrier, inc=1, device_id={"agg": lax.rem(me + d, n_agg)}, device_id_type=mesh_id)
     low = lax.broadcasted_iota(jnp.int32, (half, lanes), 1) < size
     low2 = lax.broadcasted_iota(jnp.int32, (size, lanes), 1) < size
 
@@ -256,33 +221,60 @@
     base = dev * elems
     hop = n_agg * elems
 
-    def group(g, carry):
-        total[...] = jnp.zeros_like(total)
+    def group(g, out_ref):
         for t in range(per_agg):
             e = order[g * per_agg + t]
-            stack[pl.ds(t * half, half), :] = own_ref[e]
+            part = pl.ds(t * half, half)
+            stack[part, :] = own_ref[e]
+            slots = [None] * KC
             for k in range(KC):
                 x = cols_ref[k, e] - base
                 c = jnp.where(x < 0, x + hop - (elems - face),
                               jnp.where(x >= elems, x - hop + face + elems, x + face))
                 hp = jnp.dot(h_ref[e, k], dense[c], preferred_element_type=jnp.float32)
-                total[slot_ref[k, e], pl.ds(t * half, half), :] += hp
+                slot = slot_ref[k, e]
+                for j in range(KC):
+                    own_part = hp * jnp.where(slot == j, 1.0, 0.0)
+                    slots[j] = own_part if k == 0 else slots[j] + own_part
+            for j in range(KC):
+                sums[part, j * lanes:(j + 1) * lanes] = slots[j].astype(jnp.bfloat16)
         left = stack[...].T
         for j in range(0, KC, 2):
-            if j + 1 < KC:
-                right = jnp.concatenate([total[j], total[j + 1]], axis=1).astype(jnp.bfloat16)
-            else:
-                right = total[j].astype(jnp.bfloat16)
-            r = jnp.dot(left, right, preferred_element_type=jnp.float32)
+            wide = min(2, KC - j) * lanes
+            r = jnp.dot(left, sums[:, j * lanes:j * lanes + wide], preferred_element_type=jnp.float32)
             a_top, a_bot = r[:size, :lanes], r[size:, :lanes]
             if j + 1 < KC:
                 b_top, b_bot = r[:size, lanes:], r[size:, lanes:]
                 out = jnp.where(low2, a_top, b_bot) + swap_halves(jnp.where(low2, b_top, a_bot))
             else:
                 out = jnp.where(low2, a_top + swap_halves(a_bot), within[g].astype(jnp.float32))
-            o_ref[g, j // 2] = out.astype(o_ref.dtype)
+            out_ref[g, j // 2] = out.astype(o_ref.dtype)
+
+    def sending(i):
+        peer = lax.rem(me + 1 + i, n_agg)
+        return pltpu.make_async_remote_copy(
+            src_ref=rows.at[pl.ds(peer * cap, cap)], dst_ref=o_ref.at[pl.ds(me * cap, cap)],
+            send_sem=send_sems.at[i], recv_sem=recv_sems.at[i],
+            device_id={"agg": peer}, device_id_type=mesh_id)
+
+    def to_owner(i, carry):
+        peer = lax.rem(me + 1 + i, n_agg)
+
+        def one(c, inner):
+            group(peer * cap + c, rows)
+            return inner
+        lax.fori_loop(0, cap, one, 0)
+        sending(i).start()
         return carry
-    lax.fori_loop(0, groups, group, 0)
+    pl.semaphore_wait(barrier, n_agg - 1)
+    lax.fori_loop(0, n_agg - 1, to_owner, 0)
+
+    def one(c, inner):
+        group(me * cap + c, o_ref)
+        return inner
+    lax.fori_loop(0, cap, one, 0)
+    for i in range(n_agg - 1):
+        sending(i).wait()
 
 
 def galerkin(n_agg, dev, cols, slots, order, within, h, before, own, after):
@@ -300,9 +292,13 @@
         scratch_shapes=[
             pltpu.VMEM((elems + 2 * face, lanes, lanes), jnp.bfloat16),
             pltpu.VMEM((elems // aggs * half, lanes), jnp.bfloat16),
-            pltpu.VMEM((KC, elems // aggs * half, lanes), jnp.float32),
+            pltpu.VMEM((elems // aggs * half, KC * lanes), jnp.bfloat16),
+            pltpu.VMEM((aggs, tiles, lanes // 2, lanes), jnp.bfloat16),
+            pltpu.SemaphoreType.DMA((n_agg,)),
+            pltpu.SemaphoreType.DMA((n_agg,)),
         ],
-        compiler_params=pltpu.CompilerParams(vmem_limit_bytes=VMEM_LIMIT),
+        compiler_params=pltpu.CompilerParams(
+            vmem_limit_bytes=VMEM_LIMIT, collective_id=1, has_side_effects=True),
     )(dev, cols, slots, order, within, h, before, own, after)
 
 
@@ -343,7 +339,7 @@
     h, before, after = prepare(h_blocks.transpose(1, 2, 3, 0), own)
     rows = galerkin(n_agg, device.reshape(1).astype(jnp.int32), h_cols.T, term_slot.T,
                     order, within, h, before, own, after)
-    return placed_rows(exchanged(n_agg, rows))
+    return placed_rows(rows)
 
 
 def solution(mesh):

time: 51 us -> 39.3 us (0.77)
  the two profiles are of different devices: /device:TPU:0 before, /device:TPU:3 now
where the time goes in v4:
time: 39.3 us; the launch traced here: 39.1 us
  Pallas kernels  36.5 us (93%)
  local copies, waits for them, and re-layouts  2.57 us (7%)
    pallas_call x1, Pallas kernels, galerkin(): pl.pallas_call(functools.partial(galerkin_kernel, n_agg), in_specs=[smem]...  22.7 us
    pallas_call x1, Pallas kernels, prepare(): pl.pallas_call(prepare_kernel, in_specs=[pl.BlockSpec(memory_space=pl.ANY...  9.34 us
    unnamed x10, local copies, waits for them, and re-layouts  2.57 us
    pallas_call x1, Pallas kernels, placed_rows(): pl.pallas_call(place_kernel, in_specs=[pl.BlockSpec(memory_space=pltpu.VM...  2.32 us
    pallas_call x1, Pallas kernels, sort_and_pair(): pl.pallas_call(functools.partial(sort_and_pair_kernel, n_agg), in_specs=[...  2.11 us

profile of v4, /device:TPU:3, one launch (start us, length us, event | category | flops | bytes accessed | tf_op | source)
XLA Modules:
  0.0 39.1 jit_solution(3801912824272199402)
XLA Ops:
  0.0 0.0 copy-start.2
  0.0 0.0 copy-start.1
  0.0 0.0 copy-start
  0.0 1.2 %copy-done = bf16[128,64,64]{0,2,1:T(8,128)(2,1)S(1)} copy-done((bf16[128,64,64]{0,2,1:T(8,128)(2,1)S(1)}, bf16[128,64,64]{0,2,1:T(8,128)(2,1)}, u32[]{:S(2)}) %copy-start) | copy-done | bytes 1048600
  1.3 0.0 copy-start.3
  1.3 0.7 %copy-done.3 = s32[128]{0:T(128)S(1)} copy-done((s32[128]{0:T(128)S(1)}, s32[128]{0:T(128)}, u32[]{:S(2)}) %copy-start.3) | copy-done | bytes 536
  1.9 0.0 copy-start.4
  1.9 0.7 %copy-done.4 = s32[16]{0:T(128)S(1)} copy-done((s32[16]{0:T(128)S(1)}, s32[16]{0:T(128)}, u32[]{:S(2)}) %copy-start.4) | copy-done | bytes 88
  2.6 2.1 %shard_map.64 = (bf16[128,32,128]{2,1,0:T(8,128)(2,1)S(1)}, s32[128]{0:T(128)S(1)}, s32[16]{0:T(128)S(1)}) custom-call(s32[128]{0:T(128)S(1)} %copy-done.3, s32[16]{0:T(128)S(1)} %copy-done.4, bf16[64,64,128]{2,1,0:T(8,128)(2,1)S(1)} %bitcast.5), custom_call_target="tpu_custom_call" | custom-call | tf_op jit(solution)/shard_map/pallas_call | solution.py:68
  4.7 9.3 %shard_map.65 = (bf16[128,7,32,128]{3,2,1,0:T(8,128)(2,1)S(1)}, bf16[32,32,128]{2,1,0:T(8,128)(2,1)S(1)}, bf16[32,32,128]{2,1,0:T(8,128)(2,1)S(1)}) custom-call(bf16[7,64,64,128]{3,2,1,0:T(8,128)(2,1)} %bitcast.8, bf16[128,32,128]{2,1,0:T(8,128)(2,1)S(1)} %get-tuple-element.13.own_ref), custom_call_target="tpu_custom_call" | custom-call | tf_op jit(solution)/shard_map/pallas_call | solution.py:165
  14.0 0.0 copy-done.2
  14.0 0.0 copy-done.1
  14.1 22.7 %shard_map.66.x_ref = bf16[16,4,64,128]{3,2,1,0:T(8,128)(2,1)S(1)} custom-call(s32[1]{0:T(128)} %bitcast.dev_ref, s32[7,128]{1,0:T(8,128)S(1)} %bitcast.6, s32[7,128]{1,0:T(8,128)S(1)} %bitcast.7, s32[128]{0:T(128)S(1)} %get-tuple-element.11.order, s32[16]{0:T(128)S(1)} %get-tuple-element.12.within, bf16[128,7,32,128]{3,2,1,0:T(8,128)(2,1)S(1)} %get-tuple-element.14.h_ref, ...), custom_call_target="tpu_custom_call" | custom-call | tf_op jit(solution)/shard_map/pallas_call | solution.py:287
  36.8 2.3 %shard_map.67 = bf16[16,7,64,64]{3,2,1,0:T(8,128)(2,1)} custom-call(bf16[16,4,64,128]{3,2,1,0:T(8,128)(2,1)S(1)} %shard_map.66.x_ref), custom_call_target="tpu_custom_call" | custom-call | tf_op jit(solution)/shard_map/pallas_call | solution.py:325
Async XLA Ops:
  0.0 14.0 %copy-start.2 = (s32[128,7]{0,1:T(8,128)S(1)}, s32[128,7]{0,1:T(8,128)}, u32[]{:S(2)}) copy-start(s32[128,7]{0,1:T(8,128)} %param.10) | copy-start | bytes 10756
  0.0 14.0 %copy-start.1 = (s32[128,7]{0,1:T(8,128)S(1)}, s32[128,7]{0,1:T(8,128)}, u32[]{:S(2)}) copy-start(s32[128,7]{0,1:T(8,128)} %param.7) | copy-start | bytes 10756
  0.0 1.3 %copy-start = (bf16[128,64,64]{0,2,1:T(8,128)(2,1)S(1)}, bf16[128,64,64]{0,2,1:T(8,128)(2,1)}, u32[]{:S(2)}) copy-start(bf16[128,64,64]{0,2,1:T(8,128)(2,1)} %param.8) | copy-start | bytes 3145732
  1.3 0.7 %copy-start.3 = (s32[128]{0:T(128)S(1)}, s32[128]{0:T(128)}, u32[]{:S(2)}) copy-start(s32[128]{0:T(128)} %agg_ref.1) | copy-start | bytes 1540
  1.9 0.7 %copy-start.4 = (s32[16]{0:T(128)S(1)}, s32[16]{0:T(128)}, u32[]{:S(2)}) copy-start(s32[16]{0:T(128)} %owner_ref.1) | copy-start | bytes 196
